TPU v7x, 512 devices: a whole 4x8x8 slice. The times are simulated.
512 devices in a mesh: layer: 8 (over y), row: 16 (over z, core), col: 4 (over x).
Axes of the slice: x: 4, y: 8, z: 8, core: 2. Of those that a mesh axis runs over, the one named last changes fastest.
Arguments:
- front_inv: float32 [8, 6144, 4, 1536], P('layer', 'row', 'col'), may hold values from -0.078125 to 0.078125
- impedance: float32 [8, 6144], P('layer', ('row', 'col')), may hold values from 0.3 to 1
- sources: float32 [8, 3, 4, 1536, 128], P('layer', None, 'col'), may hold values from -6 to 6
Outputs:
- outgoing: float32 [8, 3, 6144, 128], P('layer', None, ('row', 'col'))
All inputs are finite; a program needn't handle non-finite values.
Results may differ from a plain program's by a relative error of at most 0.0001.
Values sent between devices are 32-bit elements; how exact they have to be, the bound alone decides.
A program may use at most 64 MiB of HBM per device.

v0:
```python
import jax
import jax.numpy as jnp
from jax import lax
from jax.sharding import PartitionSpec as P


def passed_along(array, axis, by):
    peers = lax.axis_size(axis)
    pairs = [(i, i + by) for i in range(peers) if 0 <= i + by < peers]
    return lax.ppermute(array, axis, pairs)


def body(front_inv, impedance, sources):
    front_tile = front_inv[0, :, 0, :]
    row_scale = impedance[0][:, None]
    own_blocks = sources[0, :, 0]
    blocks = own_blocks.shape[0]
    columns_b = own_blocks.shape[2]
    rows_mine = impedance.shape[1]
    sections = lax.axis_size("layer")
    section_index = lax.axis_index("layer")

    def accumulate(gathered):
        return jnp.dot(
            front_tile,
            gathered,
            precision=lax.Precision.HIGHEST,
            preferred_element_type=jnp.float32,
        )

    def one_tick(tick, carry):
        incoming_vec, result = carry
        block_now = tick - section_index
        active = jnp.logical_and(block_now >= 0, block_now < blocks)
        block_index = jnp.clip(block_now, 0, blocks - 1)
        own_now = lax.dynamic_index_in_dim(own_blocks, block_index, 0, keepdims=False)
        partial_sum = accumulate(own_now + lax.all_gather(incoming_vec, "row", axis=0, tiled=True))
        shared = lax.psum_scatter(partial_sum, "col", scatter_dimension=0, tiled=True) * row_scale
        updated = lax.dynamic_update_index_in_dim(result, shared, block_index, 0)
        result = jnp.where(active, updated, result)
        incoming_vec = passed_along(shared, "layer", 1)
        return (incoming_vec, result)

    start_carry = (
        jnp.zeros((rows_mine, columns_b), jnp.float32),
        jnp.zeros((blocks, rows_mine, columns_b), jnp.float32),
    )
    final_carry = lax.fori_loop(0, sections + blocks - 1, one_tick, start_carry)
    return final_carry[1][None]


def solution(mesh):
    in_specs = (
        P("layer", "row", "col", None),
        P("layer", ("row", "col")),
        P("layer", None, "col", None, None),
    )
    out_specs = P("layer", None, ("row", "col"), None)
    return jax.shard_map(body, mesh=mesh, in_specs=in_specs, out_specs=out_specs, check_vma=False)
```

profile of v0, /device:TPU:57, one launch (start us, length us, event | category | flops | bytes accessed | tf_op | source)
XLA Modules:
  0.0 582.4 jit_solution(14272551068163739823)
XLA Ops:
  6.5 1.8 copy.15
  8.4 566.5 %while.15 = (s32[]{:T(128)}, f32[96,128]{0,1:T(8,128)S(1)}, f32[3,96,128]{2,1,0:T(8,128)S(1)}, s32[]{:T(128)}, f32[3,1536,128]{2,1,0:T(8,128)}, /*index=5*/f32[3...) while((s32[]{:T(128)}, f32[96,128]{0,1:T(8,128)S(1)}, ...), condition=%wide.region_2.3_spmd, body=%wide.region_0.2_spmd.sunk | while | flops 906190848 | bytes 7078531 | solution.py:48
  8.5 25.8 %all_gather.8 = f32[1536,128]{1,0:T(8,128)S(1)} all-gather(f32[96,128]{1,0:T(8,128)S(1)} %copy.22), channel_id=1, replica_groups=mesh['layer'=8,'row'=16,'col'=4] {'row'}, dimensions={0}, use_global_device_ids=true | all-gather | bytes 835584 | tf_op jit(solution)/shard_map/while/body/eval_jaxpr/all_gather | solution.py:37
  34.4 3.8 convolution_bitcast_fusion.2
  39.2 19.6 %reduce-scatter.6.cloned.1.call-done = f32[96,128]{1,0:T(8,128)} async-done(((f32[384,128]{1,0:T(8,128)}), f32[96,128]{1,0:T(8,128)}) %reduce-scatter.6.cloned.1.call-update) | async-done | bytes 49168 | tf_op jit(solution)/shard_map/while
  58.7 0.9 copy.24
  60.4 1.3 collective-permute-start
  61.7 3.7 collective-permute-done
  65.5 24.1 %all_gather.8 = f32[1536,128]{1,0:T(8,128)S(1)} all-gather(f32[96,128]{1,0:T(8,128)S(1)} %copy.22), channel_id=1, replica_groups=mesh['layer'=8,'row'=16,'col'=4] {'row'}, dimensions={0}, use_global_device_ids=true | all-gather | bytes 835584 | tf_op jit(solution)/shard_map/while/body/eval_jaxpr/all_gather | solution.py:37
  89.6 3.8 convolution_bitcast_fusion.2
  93.4 0.8 copy.23
  94.4 20.9 %reduce-scatter.6.cloned.1.call-done = f32[96,128]{1,0:T(8,128)} async-done(((f32[384,128]{1,0:T(8,128)}), f32[96,128]{1,0:T(8,128)}) %reduce-scatter.6.cloned.1.call-update) | async-done | bytes 49168 | tf_op jit(solution)/shard_map/while
  115.3 0.9 copy.24
  117.0 1.3 collective-permute-start
  118.3 3.7 collective-permute-done
  122.1 24.1 %all_gather.8 = f32[1536,128]{1,0:T(8,128)S(1)} all-gather(f32[96,128]{1,0:T(8,128)S(1)} %copy.22), channel_id=1, replica_groups=mesh['layer'=8,'row'=16,'col'=4] {'row'}, dimensions={0}, use_global_device_ids=true | all-gather | bytes 835584 | tf_op jit(solution)/shard_map/while/body/eval_jaxpr/all_gather | solution.py:37
  146.2 3.8 convolution_bitcast_fusion.2
  150.0 0.8 copy.23
  151.0 20.9 %reduce-scatter.6.cloned.1.call-done = f32[96,128]{1,0:T(8,128)} async-done(((f32[384,128]{1,0:T(8,128)}), f32[96,128]{1,0:T(8,128)}) %reduce-scatter.6.cloned.1.call-update) | async-done | bytes 49168 | tf_op jit(solution)/shard_map/while
  171.9 0.9 copy.24
  173.6 1.3 collective-permute-start
  174.9 3.7 collective-permute-done
  178.7 24.1 %all_gather.8 = f32[1536,128]{1,0:T(8,128)S(1)} all-gather(f32[96,128]{1,0:T(8,128)S(1)} %copy.22), channel_id=1, replica_groups=mesh['layer'=8,'row'=16,'col'=4] {'row'}, dimensions={0}, use_global_device_ids=true | all-gather | bytes 835584 | tf_op jit(solution)/shard_map/while/body/eval_jaxpr/all_gather | solution.py:37
  202.8 3.8 convolution_bitcast_fusion.2
  207.6 20.9 %reduce-scatter.6.cloned.1.call-done = f32[96,128]{1,0:T(8,128)} async-done(((f32[384,128]{1,0:T(8,128)}), f32[96,128]{1,0:T(8,128)}) %reduce-scatter.6.cloned.1.call-update) | async-done | bytes 49168 | tf_op jit(solution)/shard_map/while
  228.6 0.9 copy.24
  230.2 1.3 collective-permute-start
  231.5 3.7 collective-permute-done
  235.3 24.1 %all_gather.8 = f32[1536,128]{1,0:T(8,128)S(1)} all-gather(f32[96,128]{1,0:T(8,128)S(1)} %copy.22), channel_id=1, replica_groups=mesh['layer'=8,'row'=16,'col'=4] {'row'}, dimensions={0}, use_global_device_ids=true | all-gather | bytes 835584 | tf_op jit(solution)/shard_map/while/body/eval_jaxpr/all_gather | solution.py:37
  259.4 3.8 convolution_bitcast_fusion.2
  264.2 20.9 %reduce-scatter.6.cloned.1.call-done = f32[96,128]{1,0:T(8,128)} async-done(((f32[384,128]{1,0:T(8,128)}), f32[96,128]{1,0:T(8,128)}) %reduce-scatter.6.cloned.1.call-update) | async-done | bytes 49168 | tf_op jit(solution)/shard_map/while
  285.2 0.9 copy.24
  286.8 1.3 collective-permute-start
  288.2 3.7 collective-permute-done
  291.9 24.1 %all_gather.8 = f32[1536,128]{1,0:T(8,128)S(1)} all-gather(f32[96,128]{1,0:T(8,128)S(1)} %copy.22), channel_id=1, replica_groups=mesh['layer'=8,'row'=16,'col'=4] {'row'}, dimensions={0}, use_global_device_ids=true | all-gather | bytes 835584 | tf_op jit(solution)/shard_map/while/body/eval_jaxpr/all_gather | solution.py:37
  316.0 3.8 convolution_bitcast_fusion.2
  320.8 21.0 %reduce-scatter.6.cloned.1.call-done = f32[96,128]{1,0:T(8,128)} async-done(((f32[384,128]{1,0:T(8,128)}), f32[96,128]{1,0:T(8,128)}) %reduce-scatter.6.cloned.1.call-update) | async-done | bytes 49168 | tf_op jit(solution)/shard_map/while
  341.8 0.9 copy.24
  343.4 1.3 collective-permute-start
  344.8 3.7 collective-permute-done
  348.5 24.1 %all_gather.8 = f32[1536,128]{1,0:T(8,128)S(1)} all-gather(f32[96,128]{1,0:T(8,128)S(1)} %copy.22), channel_id=1, replica_groups=mesh['layer'=8,'row'=16,'col'=4] {'row'}, dimensions={0}, use_global_device_ids=true | all-gather | bytes 835584 | tf_op jit(solution)/shard_map/while/body/eval_jaxpr/all_gather | solution.py:37
  372.7 3.8 convolution_bitcast_fusion.2
  377.5 20.9 %reduce-scatter.6.cloned.1.call-done = f32[96,128]{1,0:T(8,128)} async-done(((f32[384,128]{1,0:T(8,128)}), f32[96,128]{1,0:T(8,128)}) %reduce-scatter.6.cloned.1.call-update) | async-done | bytes 49168 | tf_op jit(solution)/shard_map/while
  398.4 0.9 copy.24
  400.0 1.3 collective-permute-start
  401.4 3.7 collective-permute-done
  405.1 24.1 %all_gather.8 = f32[1536,128]{1,0:T(8,128)S(1)} all-gather(f32[96,128]{1,0:T(8,128)S(1)} %copy.22), channel_id=1, replica_groups=mesh['layer'=8,'row'=16,'col'=4] {'row'}, dimensions={0}, use_global_device_ids=true | all-gather | bytes 835584 | tf_op jit(solution)/shard_map/while/body/eval_jaxpr/all_gather | solution.py:37
  429.3 3.8 convolution_bitcast_fusion.2
  434.1 20.9 %reduce-scatter.6.cloned.1.call-done = f32[96,128]{1,0:T(8,128)} async-done(((f32[384,128]{1,0:T(8,128)}), f32[96,128]{1,0:T(8,128)}) %reduce-scatter.6.cloned.1.call-update) | async-done | bytes 49168 | tf_op jit(solution)/shard_map/while
  455.0 0.9 copy.24
  456.7 1.3 collective-permute-start
  458.0 3.7 collective-permute-done
  461.8 24.1 %all_gather.8 = f32[1536,128]{1,0:T(8,128)S(1)} all-gather(f32[96,128]{1,0:T(8,128)S(1)} %copy.22), channel_id=1, replica_groups=mesh['layer'=8,'row'=16,'col'=4] {'row'}, dimensions={0}, use_global_device_ids=true | all-gather | bytes 835584 | tf_op jit(solution)/shard_map/while/body/eval_jaxpr/all_gather | solution.py:37
  485.9 3.8 convolution_bitcast_fusion.2
  490.7 20.9 %reduce-scatter.6.cloned.1.call-done = f32[96,128]{1,0:T(8,128)} async-done(((f32[384,128]{1,0:T(8,128)}), f32[96,128]{1,0:T(8,128)}) %reduce-scatter.6.cloned.1.call-update) | async-done | bytes 49168 | tf_op jit(solution)/shard_map/while
  511.6 0.9 copy.24
  513.3 1.3 collective-permute-start
  514.6 3.7 collective-permute-done
  518.4 24.1 %all_gather.8 = f32[1536,128]{1,0:T(8,128)S(1)} all-gather(f32[96,128]{1,0:T(8,128)S(1)} %copy.22), channel_id=1, replica_groups=mesh['layer'=8,'row'=16,'col'=4] {'row'}, dimensions={0}, use_global_device_ids=true | all-gather | bytes 835584 | tf_op jit(solution)/shard_map/while/body/eval_jaxpr/all_gather | solution.py:37
  542.5 3.8 convolution_bitcast_fusion.2
  547.3 21.0 %reduce-scatter.6.cloned.1.call-done = f32[96,128]{1,0:T(8,128)} async-done(((f32[384,128]{1,0:T(8,128)}), f32[96,128]{1,0:T(8,128)}) %reduce-scatter.6.cloned.1.call-update) | async-done | bytes 49168 | tf_op jit(solution)/shard_map/while
  568.2 0.9 copy.24
  569.9 1.3 collective-permute-start
  571.2 3.7 collective-permute-done
  (92 shorter events, 16.8 us)
Async XLA Ops:
  8.4 50.3 %reduce-scatter.6.cloned.1.call-start = ((), (), s32[]{:S(2)}) async-start(), calls=%async_computation.1 | async-start | bytes 245760 | tf_op jit(solution)/shard_map/while
  60.4 5.0 collective-permute-start
  65.4 49.9 %reduce-scatter.6.cloned.1.call-start = ((), (), s32[]{:S(2)}) async-start(), calls=%async_computation.1 | async-start | bytes 245760 | tf_op jit(solution)/shard_map/while
  117.0 5.0 collective-permute-start
  122.0 49.9 %reduce-scatter.6.cloned.1.call-start = ((), (), s32[]{:S(2)}) async-start(), calls=%async_computation.1 | async-start | bytes 245760 | tf_op jit(solution)/shard_map/while
  173.6 5.0 collective-permute-start
  178.6 49.9 %reduce-scatter.6.cloned.1.call-start = ((), (), s32[]{:S(2)}) async-start(), calls=%async_computation.1 | async-start | bytes 245760 | tf_op jit(solution)/shard_map/while
  230.2 5.0 collective-permute-start
  235.2 50.0 %reduce-scatter.6.cloned.1.call-start = ((), (), s32[]{:S(2)}) async-start(), calls=%async_computation.1 | async-start | bytes 245760 | tf_op jit(solution)/shard_map/while
  286.8 5.0 collective-permute-start
  291.9 49.9 %reduce-scatter.6.cloned.1.call-start = ((), (), s32[]{:S(2)}) async-start(), calls=%async_computation.1 | async-start | bytes 245760 | tf_op jit(solution)/shard_map/while
  343.4 5.0 collective-permute-start
  348.5 49.9 %reduce-scatter.6.cloned.1.call-start = ((), (), s32[]{:S(2)}) async-start(), calls=%async_computation.1 | async-start | bytes 245760 | tf_op jit(solution)/shard_map/while
  400.0 5.0 collective-permute-start
  405.1 49.9 %reduce-scatter.6.cloned.1.call-start = ((), (), s32[]{:S(2)}) async-start(), calls=%async_computation.1 | async-start | bytes 245760 | tf_op jit(solution)/shard_map/while
  456.7 5.0 collective-permute-start
  461.7 50.0 %reduce-scatter.6.cloned.1.call-start = ((), (), s32[]{:S(2)}) async-start(), calls=%async_computation.1 | async-start | bytes 245760 | tf_op jit(solution)/shard_map/while
  513.3 5.0 collective-permute-start
  518.3 49.9 %reduce-scatter.6.cloned.1.call-start = ((), (), s32[]{:S(2)}) async-start(), calls=%async_computation.1 | async-start | bytes 245760 | tf_op jit(solution)/shard_map/while
  569.9 5.0 collective-permute-start
  574.9 0.7 copy-start
Sparse Core Ops, SparseCore 0:
  39.2 19.5 reduce-scatter.5
  94.4 20.8 reduce-scatter.5
  151.0 20.8 reduce-scatter.5
  207.6 20.8 reduce-scatter.5
  264.2 20.8 reduce-scatter.5
  320.8 20.9 reduce-scatter.5
  377.5 20.8 reduce-scatter.5
  434.1 20.8 reduce-scatter.5
  490.7 20.8 reduce-scatter.5
  547.3 20.9 reduce-scatter.5
where the time goes:
time: 589 us; the launch traced here: 582 us
  waiting for transfers between devices  245 us (42%)
  blocking collectives  243 us (41%)
  matrix products  38.4 us (7%)
  local copies, waits for them, and re-layouts  22.1 us (4%)
  between operations  13.4 us (2%)
  starting transfers between devices  13 us (2%)
  other arithmetic  6.73 us (1%)
    all_gather x10, blocking collectives, one_tick(): lax.all_gather(incoming_vec, 'row', axis=0, tiled=True)  243 us
    while x20, waiting for transfers between devices  208 us
    dot_general x10, matrix products, accumulate(): jnp.dot(front_tile, gathered, precision=lax.Precision.HIGHEST, preferred_...  38.4 us
    ppermute x10, waiting for transfers between devices, passed_along(): return lax.ppermute(array, axis, pairs)  36.9 us
    while x20, local copies, waits for them, and re-layouts  16.9 us
    ppermute x10, starting transfers between devices, passed_along(): return lax.ppermute(array, axis, pairs)  12.9 us
  transfers between devices with their start and end apart: 20, of which 20 were waited for; matrix products, arithmetic and copies ran while one was open for 0% of the time, Pallas kernels for 0%

commit v1 on v0

v1 whole, which is shorter than its diff:
```python
import functools

import jax
import jax.numpy as jnp
from jax import lax
from jax.experimental import pallas as pl
from jax.experimental.pallas import tpu as pltpu
from jax.sharding import PartitionSpec as P

MESH = pl.DeviceIdType.MESH
F32, BF16 = jnp.float32, jnp.bfloat16
LANES = 128
GROUPS = 4
WIDE = LANES // GROUPS
LAG = 2


def pick(parts):
    group = lax.broadcasted_iota(jnp.int32, parts[0].shape, 1) // WIDE
    result = parts[0]
    for g in range(1, GROUPS):
        result = jnp.where(group == g, parts[g], result)
    return result


def turned(x, by):
    by = by % GROUPS
    return x if by == 0 else pltpu.roll(x, by * WIDE, 1)


def swapped(parts):
    return [pick([turned(parts[a], a - b) for a in range(GROUPS)]) for b in range(GROUPS)]


def sweep(sizes, front, impedance, sources, out, m_own, m_other, m_parts, src, own, ag_in, vec, rs_out, rs_in, ag_out,
          from_other, scale, load_sem, swap_send, swap_recv, rs_send, rs_recv, ag_send, ag_recv, out_send, out_recv):
    layers, chips, cols = sizes
    layer, row, col = lax.axis_index("layer"), lax.axis_index("row"), lax.axis_index("col")
    z, core = row // 2, lax.rem(row, 2)
    half = chips // 2
    owner_core = z // half
    is_owner = core == owner_core
    blocks, _, _ = out.shape
    shard = impedance.shape[1]
    sub = shard // GROUPS
    chunks = blocks * GROUPS
    rows = m_own.shape[0]
    depth = m_own.shape[1]
    sibling = (layer, z * 2 + 1 - core, col)

    def owner_of(x):
        return (layer, z * 2 + owner_core, x)

    barrier = pltpu.get_barrier_semaphore()

    def greet(device):
        pl.semaphore_signal(barrier, inc=1, device_id=device, device_id_type=MESH)

    greet(sibling)

    @pl.when(is_owner)
    def _():
        for d in range(1, cols):
            x = lax.rem(col + d, cols)
            greet((layer, z * 2, x))
            greet((layer, z * 2 + 1, x))

    @pl.when(layer > 0)
    def _():
        for k in range(half):
            greet((layer - 1, (core * half + k) * 2 + core, col))

    mine = pl.multiple_of(core * depth, LANES)
    others = pl.multiple_of((1 - core) * depth, LANES)
    load_src = pltpu.make_async_copy(sources.at[:, pl.ds(mine, depth)], src, load_sem.at[0])
    load_m = pltpu.make_async_copy(front.at[:, pl.ds(mine, depth)], m_own, load_sem.at[1])
    load_m.start()
    load_src.start()

    eye = lax.broadcasted_iota(jnp.int32, (shard, shard), 0) == lax.broadcasted_iota(jnp.int32, (shard, shard), 1)
    column = jnp.sum(jnp.where(eye, jnp.broadcast_to(impedance[...], (shard, shard)), 0.0), axis=1, keepdims=True)
    column = jnp.broadcast_to(column, (shard, LANES))
    scale[core] = pick([column[g * sub : (g + 1) * sub] for g in range(GROUPS)])

    sends_on = jnp.logical_and(is_owner, layer < layers - 1)

    @pl.when(sends_on)
    def _():
        pl.semaphore_wait(barrier, cols + chips)

    @pl.when(jnp.logical_not(sends_on))
    def _():
        pl.semaphore_wait(barrier, cols)

    swap_m = pltpu.make_async_remote_copy(
        src_ref=front.at[:, pl.ds(others, depth)], dst_ref=m_other, send_sem=swap_send.at[0], recv_sem=swap_recv.at[0],
        device_id=sibling, device_id_type=MESH)
    swap_m.start()
    swap_s = pltpu.make_async_remote_copy(
        src_ref=scale.at[core], dst_ref=scale.at[core], send_sem=swap_send.at[1], recv_sem=swap_recv.at[1],
        device_id=sibling, device_id_type=MESH)
    swap_s.start()

    load_src.wait()

    def pack_own(i, _):
        b, p = i // (2 * half), lax.rem(i, 2 * half)
        parts = [src[b, pl.ds(pl.multiple_of(p * shard + g * sub, 8), sub)] for g in range(GROUPS)]
        for q, packed in enumerate(swapped(parts)):
            own[b * GROUPS + q, pl.ds(pl.multiple_of(p * sub, 8), sub)] = packed
        return 0

    lax.fori_loop(0, blocks * 2 * half, pack_own, 0)

    @pl.when(layer == 0)
    def _():
        ag_in[...] = jnp.zeros_like(ag_in)

    def split(source, at):
        whole = source[...]
        high = whole.astype(BF16)
        m_parts[pl.ds(pl.multiple_of(at * rows, 16), rows)] = high
        m_parts[pl.ds(pl.multiple_of((2 + at) * rows, 16), rows)] = (whole - high.astype(F32)).astype(BF16)

    load_m.wait()
    split(m_own, core)
    swap_m.wait_recv()
    split(m_other, 1 - core)
    swap_s.wait_recv()

    def product(j):
        @pl.when(layer > 0)
        def _():
            pltpu.make_async_copy(ag_in.at[j], ag_in.at[j], ag_recv.at[j]).wait()

        total = own[j] + ag_in[j]
        high = total.astype(BF16).astype(F32)
        low = total - high
        highs = [turned(high, d) for d in range(GROUPS)]
        lows = [turned(low, d) for d in range(GROUPS)]
        for g in range(GROUPS):
            spread = pick([(lows if q % 2 else highs)[(q - g) % GROUPS] for q in range(GROUPS)])
            for p in range(2 * half):
                vec[pl.ds(p * shard + g * sub, sub)] = spread[p * sub : (p + 1) * sub]
        result = jnp.dot(m_parts[...], vec[...].astype(BF16), preferred_element_type=F32)
        summed = result[: 2 * rows] + result[2 * rows :]
        summed = summed + pltpu.roll(summed, WIDE, 1)
        for q in range(cols):
            for t in range(2):
                at = t * rows + q * shard
                rs_out[j, q, pl.ds(t * sub, sub)] = pick([summed[at + g * sub : at + (g + 1) * sub] for g in range(GROUPS)])
        for d in (2, 1, 3):
            x = lax.rem(col + d, cols)
            pltpu.make_async_remote_copy(
                src_ref=rs_out.at[j, x], dst_ref=rs_in.at[j, col * 2 + core], send_sem=rs_send, recv_sem=rs_recv.at[j],
                device_id=owner_of(x), device_id_type=MESH).start()

        @pl.when(jnp.logical_not(is_owner))
        def _():
            pltpu.make_async_remote_copy(
                src_ref=rs_out.at[j, col], dst_ref=rs_in.at[j, col * 2 + core], send_sem=rs_send, recv_sem=rs_recv.at[j],
                device_id=sibling, device_id_type=MESH).start()

        @pl.when(is_owner)
        def _():
            rs_in[j, col * 2 + core] = rs_out[j, col]

    def hand_on(j):
        arrived = rs_in.at[j, pl.ds(0, 2 * cols - 1)]
        pltpu.make_async_copy(arrived, arrived, rs_recv.at[j]).wait()
        total = rs_in[j, 0]
        for s in range(1, 2 * cols):
            total = total + rs_in[j, s]
        for t in range(2):
            ag_out[j, pl.ds(t * sub, sub)] = total[t * sub : (t + 1) * sub] * scale[t]

        @pl.when(layer < layers - 1)
        def _():
            for dz in (4, 3, 5, 2, 6, 1, 7, 0):
                pltpu.make_async_remote_copy(
                    src_ref=ag_out.at[j],
                    dst_ref=ag_in.at[j, pl.ds(pl.multiple_of((z - owner_core * half) * 2 * sub, 8), 2 * sub)],
                    send_sem=ag_send, recv_sem=ag_recv.at[j],
                    device_id=(layer + 1, lax.rem(z + dz, chips) * 2 + core, col), device_id_type=MESH).start()

    def tick(j, _):
        @pl.when(j < chunks)
        def _():
            product(j)

        @pl.when(jnp.logical_and(j >= LAG, is_owner))
        def _():
            hand_on(j - LAG)

        return 0

    lax.fori_loop(0, chunks + LAG, tick, 0)

    def finish(results):
        for b in range(blocks):
            for g, part in enumerate(swapped([results[b * GROUPS + q] for q in range(GROUPS)])):
                out[b, pl.ds(g * sub, sub)] = part

    @pl.when(is_owner)
    def _():
        give = pltpu.make_async_remote_copy(
            src_ref=ag_out.at[:, pl.ds(pl.multiple_of((1 - core) * sub, 8), sub)], dst_ref=from_other,
            send_sem=out_send, recv_sem=out_recv, device_id=sibling, device_id_type=MESH)
        give.start()
        kept = pl.ds(pl.multiple_of(core * sub, 8), sub)
        finish([ag_out[j, kept] for j in range(chunks)])
        give.wait_send()
        sent = rs_out.at[:, pl.ds(0, cols - 1)]
        pltpu.make_async_copy(sent, sent, rs_send).wait()

        @pl.when(layer < layers - 1)
        def _():
            pltpu.make_async_copy(rs_in, rs_in, ag_send).wait()

    @pl.when(jnp.logical_not(is_owner))
    def _():
        pltpu.make_async_copy(from_other, from_other, out_recv).wait()
        finish([from_other[j] for j in range(chunks)])
        pltpu.make_async_copy(rs_out, rs_out, rs_send).wait()

    swap_m.wait_send()
    swap_s.wait_send()


def solution(mesh):
    layers, chips, cols = mesh.shape["layer"], mesh.shape["row"] // 2, mesh.shape["col"]

    def body(front_inv, impedance, sources):
        rows, depth = front_inv.shape[1], front_inv.shape[3] // 2
        blocks, shard = sources.shape[1], impedance.shape[1]
        chunks, sub = blocks * GROUPS, shard // GROUPS
        sems = pltpu.SemaphoreType.DMA
        result = pl.pallas_call(
            functools.partial(sweep, (layers, chips, cols)),
            out_shape=jax.ShapeDtypeStruct((blocks, shard, LANES), F32),
            in_specs=[
                pl.BlockSpec(memory_space=pl.ANY),
                pl.BlockSpec(memory_space=pltpu.VMEM),
                pl.BlockSpec(memory_space=pl.ANY),
            ],
            out_specs=pl.BlockSpec(memory_space=pltpu.VMEM),
            scratch_shapes=[
                pltpu.VMEM((rows, depth), F32),
                pltpu.VMEM((rows, depth), F32),
                pltpu.VMEM((4 * rows, depth), BF16),
                pltpu.VMEM((blocks, depth, LANES), F32),
                pltpu.VMEM((chunks, chips * sub, LANES), F32),
                pltpu.VMEM((chunks, chips * sub, LANES), F32),
                pltpu.VMEM((depth, LANES), F32),
                pltpu.VMEM((chunks, cols, 2 * sub, LANES), F32),
                pltpu.VMEM((chunks, 2 * cols, 2 * sub, LANES), F32),
                pltpu.VMEM((chunks, 2 * sub, LANES), F32),
                pltpu.VMEM((chunks, sub, LANES), F32),
                pltpu.VMEM((2, sub, LANES), F32),
                sems((2,)),
                sems((2,)),
                sems((2,)),
                sems,
                sems((chunks,)),
                sems,
                sems((chunks,)),
                sems,
                sems,
            ],
            compiler_params=pltpu.CompilerParams(
                collective_id=0, has_side_effects=True, vmem_limit_bytes=40 * 2**20
            ),
            name="front_sweep",
        )(front_inv.reshape(rows, 2 * depth), impedance, sources.reshape(blocks, 2 * depth, LANES))
        return result[None]

    in_specs = (
        P("layer", "row", "col", None),
        P("layer", ("row", "col")),
        P("layer", None, "col", None, None),
    )
    out_specs = P("layer", None, ("row", "col"), None)
    return jax.shard_map(body, mesh=mesh, in_specs=in_specs, out_specs=out_specs, check_vma=False)
```

time: 589 us -> 122 us (0.21); the launches traced: 582 us -> 122 us
  waiting for transfers between devices: 245 us -> 0 us
  blocking collectives: 243 us -> 0 us
  Pallas kernels: 0 us -> 119 us
  matrix products: 38.4 us -> 0 us
  local copies, waits for them, and re-layouts: 22.1 us -> 3.04 us
  between operations: 13.4 us -> 0.01 us
  starting transfers between devices: 13 us -> 0 us
  other arithmetic: 6.73 us -> 0 us
    all_gather x10 -> x0, blocking collectives: 243 us -> none  [one_tick(): lax.all_gather(incoming_vec, 'row', axis=0, tiled=True)]
    while x20 -> x0, waiting for transfers between devices: 208 us -> none
    pallas_call x0 -> x1, Pallas kernels: none -> 119 us  [body(): pl.pallas_call(functools.partial(sweep, (layers, chips, cols)), out_shape...]
    dot_general x10 -> x0, matrix products: 38.4 us -> none  [accumulate(): jnp.dot(front_tile, gathered, precision=lax.Precision.HIGHEST, preferred_...]
    ppermute x10 -> x0, waiting for transfers between devices: 36.9 us -> none  [passed_along(): return lax.ppermute(array, axis, pairs)]
    while x20 -> x0, local copies, waits for them, and re-layouts: 16.9 us -> none
    ppermute x10 -> x0, starting transfers between devices: 12.9 us -> none  [passed_along(): return lax.ppermute(array, axis, pairs)]
    select_n x10 -> x0, other arithmetic: 6.73 us -> none  [one_tick(): result = jnp.where(active, updated, result)]
  transfers between devices with their start and end apart: 20 -> 0, of which waited for: 20 -> 0; matrix products, arithmetic and copies ran while one was open for 0% -> 0% of each run, Pallas kernels for 0% -> 0%
where the time goes in v1:
time: 122 us
  Pallas kernels  119 us (98%)
  local copies, waits for them, and re-layouts  3.04 us (2%)
    pallas_call x1, Pallas kernels, body(): pl.pallas_call(functools.partial(sweep, (layers, chips, cols)), out_shape...  119 us
    unnamed x6, local copies, waits for them, and re-layouts  3.04 us

profile of v1, /device:TPU:57, one launch (start us, length us, event | category | flops | bytes accessed | tf_op | source)
XLA Modules:
  0.0 122.1 jit_solution(3410047004139978203)
XLA Ops:
  0.0 0.0 copy-start
  0.0 0.0 copy-start.1
  0.0 2.0 %copy.6 = f32[1,384,1,1536]{3,1,2,0:T(8,128)S(1)} copy(f32[1,384,1,1536]{3,2,1,0:T(1,128)} %param.3) | data formatting | bytes 4718592
  2.0 0.4 copy-done
  2.4 0.0 copy-done.1
  2.4 119.1 %front_sweep.1 = f32[3,96,128]{2,1,0:T(8,128)S(1)} custom-call(f32[384,1536]{1,0:T(8,128)S(1)} %bitcast.5, f32[1,96]{1,0:T(1,128)S(1)} %copy-done.1, f32[3,1536,128]{2,1,0:T(8,128)S(1)} %bitcast.6), custom_call_target="tpu_custom_call" | custom-call | tf_op jit(solution)/shard_map/front_sweep/pallas_call | solution.py:238
  121.4 0.7 copy.8
Async XLA Ops:
  0.0 2.4 %copy-start = (f32[1,3,1,1536,128]{4,3,2,1,0:T(8,128)S(1)}, f32[1,3,1,1536,128]{4,3,2,1,0:T(8,128)}, u32[]{:S(2)}) copy-start(f32[1,3,1,1536,128]{4,3,2,1,0:T(8,128)} %param.5) | copy-start | bytes 7077892
  0.0 2.4 %copy-start.1 = (f32[1,96]{1,0:T(1,128)S(1)}, f32[1,96]{1,0:T(1,128)}, u32[]{:S(2)}) copy-start(f32[1,96]{1,0:T(1,128)} %impedance.1) | copy-start | bytes 1156

commit v2 on v1

v2 whole, which is shorter than its diff:
```python
import functools

import jax
import jax.numpy as jnp
from jax import lax
from jax.experimental import pallas as pl
from jax.experimental.pallas import tpu as pltpu
from jax.sharding import PartitionSpec as P

MESH = pl.DeviceIdType.MESH
F32, BF16 = jnp.float32, jnp.bfloat16
LANES = 128
HALF = LANES // 2
WIDE = 16
LAG = 3
ORDER = (2, 1, 3, 0)


def left(x, y):
    return jnp.where(lax.broadcasted_iota(jnp.int32, x.shape, 1) < HALF, x, y)


def turned(x, by):
    return pltpu.roll(x, by, 1)


def sweep(sizes, front, impedance, sources, out, tile, m_send, full, m_parts, src, own, ag_in, rs_out, rs_in, ag_out,
          from_other, raw, scale, load_sem, swap_send, swap_recv, rs_send, rs_recv, ag_send, ag_recv, out_send, out_recv):
    layers, chips, cols = sizes
    layer, row, col = lax.axis_index("layer"), lax.axis_index("row"), lax.axis_index("col")
    z, core = row // 2, lax.rem(row, 2)
    half = chips // 2
    owner_core = z // half
    is_owner = core == owner_core
    blocks, shard, _ = out.shape
    parts_of = LANES // WIDE
    chunks = blocks * parts_of
    piece = rs_in.shape[2]
    _, rows, depth = full.shape
    lane_blocks = depth // LANES
    sibling = (layer, z * 2 + 1 - core, col)

    def owner_of(x):
        return (layer, z * 2 + owner_core, x)

    barrier = pltpu.get_barrier_semaphore()

    def greet(device):
        pl.semaphore_signal(barrier, inc=1, device_id=device, device_id_type=MESH)

    @pl.when(layer > 0)
    def _():
        for k in range(half):
            greet((layer - 1, (core * half + k) * 2 + core, col))

    @pl.when(is_owner)
    def _():
        for d in range(1, cols):
            x = lax.rem(col + d, cols)
            greet((layer, z * 2, x))
            greet((layer, z * 2 + 1, x))

    greet(sibling)

    mine = pl.multiple_of(core * depth, LANES)
    load_src = pltpu.make_async_copy(sources.at[:, pl.ds(mine, depth)], src, load_sem.at[0])
    load_m = pltpu.make_async_copy(front, tile, load_sem.at[1])
    load_m.start()
    load_src.start()

    raw[core] = jnp.zeros(raw.shape[1:], F32)
    raw[core, :, :shard] = jnp.broadcast_to(impedance[...], (raw.shape[1], shard))

    def lane_block(at_core, k):
        return tile[pl.ds(at_core * lane_blocks + k, rows, stride=2 * lane_blocks)]

    load_m.wait()
    for k in range(lane_blocks):
        m_send[:, k * LANES : (k + 1) * LANES] = lane_block(1 - core, k)
    for k in range(lane_blocks):
        full[core, :, k * LANES : (k + 1) * LANES] = lane_block(core, k)

    load_src.wait()
    for b in range(blocks):
        for k in range(lane_blocks):
            if k < half:
                picked = src[b, pl.ds(2 * shard * k, LANES)]
            else:
                first = 2 * (k - half)
                picked = jnp.concatenate([src[b, pl.ds(2 * shard * i + LANES, HALF)] for i in (first, first + 1)])
            flipped = picked.T
            for c in range(parts_of):
                own[b * parts_of + c, :, k * LANES : (k + 1) * LANES] = flipped[c * WIDE : (c + 1) * WIDE]

    @pl.when(layer == 0)
    def _():
        ag_in[...] = jnp.zeros_like(ag_in)

    sends_on = jnp.logical_and(is_owner, layer < layers - 1)

    @pl.when(sends_on)
    def _():
        pl.semaphore_wait(barrier, cols + chips)

    @pl.when(jnp.logical_not(sends_on))
    def _():
        pl.semaphore_wait(barrier, cols)

    swaps = []
    for k in range(lane_blocks):
        lanes = slice(k * LANES, (k + 1) * LANES)
        swaps.append(pltpu.make_async_remote_copy(
            src_ref=m_send.at[:, lanes], dst_ref=full.at[core, :, lanes], send_sem=swap_send.at[k],
            recv_sem=swap_recv.at[k], device_id=sibling, device_id_type=MESH))
    swaps.append(pltpu.make_async_remote_copy(
        src_ref=raw.at[core], dst_ref=raw.at[core], send_sem=swap_send.at[lane_blocks],
        recv_sem=swap_recv.at[lane_blocks], device_id=sibling, device_id_type=MESH))
    for swap in swaps:
        swap.start()

    for k in range(lane_blocks):
        swaps[k].wait_recv()
        lanes = slice(k * LANES, (k + 1) * LANES)
        for pair in range(cols // 2):
            first, second = (
                pl.multiple_of(lax.rem(col + d, cols) * shard, 8) for d in ORDER[2 * pair : 2 * pair + 2])
            over = LANES - shard
            picked = [
                jnp.concatenate([full[0, pl.ds(at, shard), lanes], full[1, pl.ds(at, over), lanes]])
                for at in (first, second)
            ]
            picked.append(jnp.concatenate([full[1, pl.ds(at + over, HALF), lanes] for at in (first, second)]))
            for n, values in enumerate(picked):
                flipped = values.T
                high = flipped.astype(BF16)
                low = (flipped - high.astype(F32)).astype(BF16)
                for g in (0, 1):
                    chip, part = divmod(2 * k + g, 3)
                    to = LANES * chip + HALF * part if part < 2 else LANES * half + HALF * chip
                    for i, kept in enumerate((high, low)):
                        at = (3 * i + n) * LANES
                        m_parts[pair, to : to + HALF, at : at + LANES] = kept[g * HALF : (g + 1) * HALF]

    swaps[lane_blocks].wait_recv()
    lane = lax.broadcasted_iota(jnp.int32, raw.shape[1:], 1)
    shifted = turned(raw[1], shard)
    for at in range(0, WIDE, raw.shape[1]):
        scale[at : at + raw.shape[1]] = jnp.where(lane < shard, raw[0], shifted)
    for at in range(WIDE, piece, raw.shape[1]):
        scale[at : at + raw.shape[1]] = left(shifted, turned(shifted, HALF))

    def product(j):
        @pl.when(layer > 0)
        def _():
            pltpu.make_async_copy(ag_in.at[j], ag_in.at[j], ag_recv.at[j]).wait()

        came = [ag_in[j, k, :WIDE] for k in range(half)]
        for k in range(0, half, 2):
            a, b = ag_in[j, k, WIDE:], ag_in[j, k + 1, WIDE:]
            came.append(jnp.concatenate([left(a, turned(b, HALF)), left(turned(a, HALF), b)]))
        total = own[j] + jnp.concatenate(came, axis=1)
        high = total.astype(BF16)
        vec = jnp.concatenate([high, (total - high.astype(F32)).astype(BF16)])
        for pair in range(cols // 2):
            result = jnp.dot(vec, m_parts[pair], preferred_element_type=F32)
            result = result[:WIDE] + result[WIDE:]
            result = result[:, : 3 * LANES] + result[:, 3 * LANES :]
            top, bottom = result[: WIDE // 2, 2 * LANES :], result[WIDE // 2 :, 2 * LANES :]
            rs_out[j, 2 * pair, :WIDE] = result[:, :LANES]
            rs_out[j, 2 * pair, WIDE:] = left(top, turned(bottom, HALF))
            rs_out[j, 2 * pair + 1, :WIDE] = result[:, LANES : 2 * LANES]
            rs_out[j, 2 * pair + 1, WIDE:] = left(turned(top, HALF), bottom)
            for n in (2 * pair, 2 * pair + 1):
                if ORDER[n]:
                    pltpu.make_async_remote_copy(
                        src_ref=rs_out.at[j, n], dst_ref=rs_in.at[j, col * 2 + core], send_sem=rs_send,
                        recv_sem=rs_recv.at[j], device_id=owner_of(lax.rem(col + ORDER[n], cols)),
                        device_id_type=MESH).start()

        @pl.when(jnp.logical_not(is_owner))
        def _():
            pltpu.make_async_remote_copy(
                src_ref=rs_out.at[j, cols - 1], dst_ref=rs_in.at[j, col * 2 + core], send_sem=rs_send,
                recv_sem=rs_recv.at[j], device_id=sibling, device_id_type=MESH).start()

        @pl.when(is_owner)
        def _():
            rs_in[j, col * 2 + core] = rs_out[j, cols - 1]

    def hand_on(j):
        arrived = rs_in.at[j, pl.ds(0, 2 * cols - 1)]
        pltpu.make_async_copy(arrived, arrived, rs_recv.at[j]).wait()
        total = rs_in[j, 0]
        for s in range(1, 2 * cols):
            total = total + rs_in[j, s]
        ag_out[j] = total * scale[...]

        @pl.when(layer < layers - 1)
        def _():
            for dz in (4, 3, 5, 2, 6, 1, 7, 0):
                pltpu.make_async_remote_copy(
                    src_ref=ag_out.at[j], dst_ref=ag_in.at[j, z - owner_core * half],
                    send_sem=ag_send, recv_sem=ag_recv.at[j],
                    device_id=(layer + 1, lax.rem(z + dz, chips) * 2 + core, col), device_id_type=MESH).start()

    def tick(j, _):
        @pl.when(j < chunks)
        def _():
            product(j)

        @pl.when(jnp.logical_and(j >= LAG, is_owner))
        def _():
            hand_on(j - LAG)

        return 0

    lax.fori_loop(0, chunks + LAG, tick, 0)

    def finish(results):
        for b in range(blocks):
            some = [results[b * parts_of + c] for c in range(parts_of)]
            first = jnp.concatenate([r[:WIDE] for r in some])
            rest = jnp.concatenate([v for r in some for v in (r[WIDE:], turned(r[WIDE:], HALF))])
            lane = lax.broadcasted_iota(jnp.int32, first.shape, 1)
            over = LANES - shard
            second = jnp.where(lane < over, turned(first, over), turned(rest, over))
            out[b] = jnp.where(core == 0, first, second).T[:shard]

    @pl.when(is_owner)
    def _():
        give = pltpu.make_async_remote_copy(
            src_ref=ag_out, dst_ref=from_other, send_sem=out_send, recv_sem=out_recv, device_id=sibling,
            device_id_type=MESH)
        give.start()
        finish([ag_out[j] for j in range(chunks)])
        give.wait_send()
        sent = rs_out.at[:, pl.ds(0, cols - 1)]
        pltpu.make_async_copy(sent, sent, rs_send).wait()

        @pl.when(layer < layers - 1)
        def _():
            pltpu.make_async_copy(rs_in, rs_in, ag_send).wait()

    @pl.when(jnp.logical_not(is_owner))
    def _():
        pltpu.make_async_copy(from_other, from_other, out_recv).wait()
        finish([from_other[j] for j in range(chunks)])
        pltpu.make_async_copy(rs_out, rs_out, rs_send).wait()

    for swap in swaps:
        swap.wait_send()


def solution(mesh):
    layers, chips, cols = mesh.shape["layer"], mesh.shape["row"] // 2, mesh.shape["col"]

    def body(front_inv, impedance, sources):
        rows, depth = front_inv.shape[1], front_inv.shape[3] // 2
        blocks, shard = sources.shape[1], impedance.shape[1]
        chunks, piece = blocks * LANES // WIDE, 2 * shard * WIDE // LANES
        sems = pltpu.SemaphoreType.DMA
        result = pl.pallas_call(
            functools.partial(sweep, (layers, chips, cols)),
            out_shape=jax.ShapeDtypeStruct((blocks, shard, LANES), F32),
            in_specs=[
                pl.BlockSpec(memory_space=pl.ANY),
                pl.BlockSpec(memory_space=pltpu.VMEM),
                pl.BlockSpec(memory_space=pl.ANY),
            ],
            out_specs=pl.BlockSpec(memory_space=pltpu.VMEM),
            scratch_shapes=[
                pltpu.VMEM((rows * 2 * depth // LANES, LANES), F32),
                pltpu.VMEM((rows, depth), F32),
                pltpu.VMEM((2, rows, depth), F32),
                pltpu.VMEM((cols // 2, depth, 2 * rows), BF16),
                pltpu.VMEM((blocks, depth, LANES), F32),
                pltpu.VMEM((chunks, WIDE, depth), F32),
                pltpu.VMEM((chunks, chips // 2, piece, LANES), F32),
                pltpu.VMEM((chunks, cols, piece, LANES), F32),
                pltpu.VMEM((chunks, 2 * cols, piece, LANES), F32),
                pltpu.VMEM((chunks, piece, LANES), F32),
                pltpu.VMEM((chunks, piece, LANES), F32),
                pltpu.VMEM((2, 8, LANES), F32),
                pltpu.VMEM((piece, LANES), F32),
                sems((2,)),
                sems((depth // LANES + 1,)),
                sems((depth // LANES + 1,)),
                sems,
                sems((chunks,)),
                sems,
                sems((chunks,)),
                sems,
                sems,
            ],
            compiler_params=pltpu.CompilerParams(
                collective_id=0, has_side_effects=True, vmem_limit_bytes=56 * 2**20
            ),
            name="front_sweep",
        )(
            front_inv.reshape(rows * 2 * depth // LANES, LANES),
            impedance,
            sources.reshape(blocks, 2 * depth, LANES),
        )
        return result[None]

    in_specs = (
        P("layer", "row", "col", None),
        P("layer", ("row", "col")),
        P("layer", None, "col", None, None),
    )
    out_specs = P("layer", None, ("row", "col"), None)
    return jax.shard_map(body, mesh=mesh, in_specs=in_specs, out_specs=out_specs, check_vma=False)
```

time: 122 us -> 110 us (0.902)
  Pallas kernels: 119 us -> 108 us
  local copies, waits for them, and re-layouts: 3.04 us -> 1.58 us
    pallas_call x1, Pallas kernels: 119 us -> 108 us  [body(): pl.pallas_call(functools.partial(sweep, (layers, chips, cols)), out_shape...]
    unnamed x6 -> x1, local copies, waits for them, and re-layouts: 3.04 us -> 1.58 us
where the time goes in v2:
time: 110 us
  Pallas kernels  108 us (98%)
  local copies, waits for them, and re-layouts  1.58 us (1%)
    pallas_call x1, Pallas kernels, body(): pl.pallas_call(functools.partial(sweep, (layers, chips, cols)), out_shape...  108 us

profile of v2, /device:TPU:57, one launch (start us, length us, event | category | flops | bytes accessed | tf_op | source)
XLA Modules:
  0.0 109.8 jit_solution(7413256530041073508)
XLA Ops:
  0.0 108.2 %front_sweep.1 = f32[3,96,128]{2,1,0:T(8,128)} custom-call(f32[4608,128]{1,0:T(8,128)} %bitcast.3, f32[1,96]{1,0:T(1,128)} %impedance.1, f32[3,1536,128]{2,1,0:T(8,128)} %bitcast.4), custom_call_target="tpu_custom_call" | custom-call | tf_op jit(solution)/shard_map/front_sweep/pallas_call | solution.py:262
  108.2 1.6 %copy.5 = f32[1,3,96,128]{3,2,1,0:T(8,128)} copy(f32[1,3,96,128]{3,2,1,0:T(8,128)} %bitcast.5) | data formatting | bytes 294912

commit v3 on v2

--- a/solution.py
+++ b/solution.py
@@ -14,6 +14,7 @@
 WIDE = 16
 LAG = 3
 ORDER = (2, 1, 3, 0)
+SPREAD = (4, 3, 5, 2, 6, 1, 7, 0)
 
 
 def left(x, y):
@@ -25,13 +26,12 @@
 
 
 def sweep(sizes, front, impedance, sources, out, tile, m_send, full, m_parts, src, own, ag_in, rs_out, rs_in, ag_out,
-          from_other, raw, scale, load_sem, swap_send, swap_recv, rs_send, rs_recv, ag_send, ag_recv, out_send, out_recv):
+          raw, scale, ready, load_sem, swap_send, swap_recv, rs_send, rs_recv, ag_send, ag_recv, out_send, out_recv):
     layers, chips, cols = sizes
     layer, row, col = lax.axis_index("layer"), lax.axis_index("row"), lax.axis_index("col")
     z, core = row // 2, lax.rem(row, 2)
     half = chips // 2
-    owner_core = z // half
-    is_owner = core == owner_core
+    half_of = z // half
     blocks, shard, _ = out.shape
     parts_of = LANES // WIDE
     chunks = blocks * parts_of
@@ -40,22 +40,23 @@
     lane_blocks = depth // LANES
     sibling = (layer, z * 2 + 1 - core, col)
 
-    def owner_of(x):
-        return (layer, z * 2 + owner_core, x)
+    is_owner = core == half_of
 
     barrier = pltpu.get_barrier_semaphore()
 
     def greet(device):
         pl.semaphore_signal(barrier, inc=1, device_id=device, device_id_type=MESH)
 
-    @pl.when(layer > 0)
-    def _():
-        for k in range(half):
-            greet((layer - 1, (core * half + k) * 2 + core, col))
+    hands_on = jnp.logical_and(is_owner, layer < layers - 1)
+
+    @pl.when(hands_on)
+    def _():
+        for dz in SPREAD:
+            greet((layer + 1, lax.rem(z + dz, chips) * 2 + core, col))
 
     @pl.when(is_owner)
     def _():
-        for d in range(1, cols):
+        for d in ORDER[:-1]:
             x = lax.rem(col + d, cols)
             greet((layer, z * 2, x))
             greet((layer, z * 2 + 1, x))
@@ -79,6 +80,33 @@
         m_send[:, k * LANES : (k + 1) * LANES] = lane_block(1 - core, k)
     for k in range(lane_blocks):
         full[core, :, k * LANES : (k + 1) * LANES] = lane_block(core, k)
+
+    @pl.when(layer == 0)
+    def _():
+        ag_in[...] = jnp.zeros_like(ag_in)
+
+    @pl.when(layer == 0)
+    def _():
+        pl.semaphore_wait(barrier, cols)
+
+    @pl.when(layer > 0)
+    def _():
+        pl.semaphore_wait(barrier, cols + half)
+        for k in range(half):
+            pl.semaphore_signal(
+                ready, inc=1, device_id=(layer - 1, (core * half + k) * 2 + core, col), device_id_type=MESH)
+
+    swaps = []
+    for k in range(lane_blocks):
+        lanes = slice(k * LANES, (k + 1) * LANES)
+        swaps.append(pltpu.make_async_remote_copy(
+            src_ref=m_send.at[:, lanes], dst_ref=full.at[core, :, lanes], send_sem=swap_send.at[k],
+            recv_sem=swap_recv.at[k], device_id=sibling, device_id_type=MESH))
+    swaps.append(pltpu.make_async_remote_copy(
+        src_ref=raw.at[core], dst_ref=raw.at[core], send_sem=swap_send.at[lane_blocks],
+        recv_sem=swap_recv.at[lane_blocks], device_id=sibling, device_id_type=MESH))
+    for swap in swaps:
+        swap.start()
 
     load_src.wait()
     for b in range(blocks):
@@ -91,32 +119,6 @@
             flipped = picked.T
             for c in range(parts_of):
                 own[b * parts_of + c, :, k * LANES : (k + 1) * LANES] = flipped[c * WIDE : (c + 1) * WIDE]
-
-    @pl.when(layer == 0)
-    def _():
-        ag_in[...] = jnp.zeros_like(ag_in)
-
-    sends_on = jnp.logical_and(is_owner, layer < layers - 1)
-
-    @pl.when(sends_on)
-    def _():
-        pl.semaphore_wait(barrier, cols + chips)
-
-    @pl.when(jnp.logical_not(sends_on))
-    def _():
-        pl.semaphore_wait(barrier, cols)
-
-    swaps = []
-    for k in range(lane_blocks):
-        lanes = slice(k * LANES, (k + 1) * LANES)
-        swaps.append(pltpu.make_async_remote_copy(
-            src_ref=m_send.at[:, lanes], dst_ref=full.at[core, :, lanes], send_sem=swap_send.at[k],
-            recv_sem=swap_recv.at[k], device_id=sibling, device_id_type=MESH))
-    swaps.append(pltpu.make_async_remote_copy(
-        src_ref=raw.at[core], dst_ref=raw.at[core], send_sem=swap_send.at[lane_blocks],
-        recv_sem=swap_recv.at[lane_blocks], device_id=sibling, device_id_type=MESH))
-    for swap in swaps:
-        swap.start()
 
     for k in range(lane_blocks):
         swaps[k].wait_recv()
@@ -174,7 +176,7 @@
                 if ORDER[n]:
                     pltpu.make_async_remote_copy(
                         src_ref=rs_out.at[j, n], dst_ref=rs_in.at[j, col * 2 + core], send_sem=rs_send,
-                        recv_sem=rs_recv.at[j], device_id=owner_of(lax.rem(col + ORDER[n], cols)),
+                        recv_sem=rs_recv.at[j], device_id=(layer, z * 2 + half_of, lax.rem(col + ORDER[n], cols)),
                         device_id_type=MESH).start()
 
         @pl.when(jnp.logical_not(is_owner))
@@ -186,6 +188,12 @@
         @pl.when(is_owner)
         def _():
             rs_in[j, col * 2 + core] = rs_out[j, cols - 1]
+
+    def give(b):
+        some = ag_out.at[pl.ds(b * parts_of, parts_of)]
+        return pltpu.make_async_remote_copy(
+            src_ref=some, dst_ref=some, send_sem=out_send.at[b], recv_sem=out_recv.at[b], device_id=sibling,
+            device_id_type=MESH)
 
     def hand_on(j):
         arrived = rs_in.at[j, pl.ds(0, 2 * cols - 1)]
@@ -197,11 +205,19 @@
 
         @pl.when(layer < layers - 1)
         def _():
-            for dz in (4, 3, 5, 2, 6, 1, 7, 0):
+            @pl.when(j == 0)
+            def _():
+                pl.semaphore_wait(ready, chips)
+
+            for dz in SPREAD:
                 pltpu.make_async_remote_copy(
-                    src_ref=ag_out.at[j], dst_ref=ag_in.at[j, z - owner_core * half],
+                    src_ref=ag_out.at[j], dst_ref=ag_in.at[j, z - half_of * half],
                     send_sem=ag_send, recv_sem=ag_recv.at[j],
-                    device_id=(layer + 1, lax.rem(z + dz, chips) * 2 + core, col), device_id_type=MESH).start()
+                    device_id=(layer + 1, lax.rem(z + dz, chips) * 2 + half_of, col), device_id_type=MESH).start()
+
+        @pl.when(lax.rem(j, parts_of) == parts_of - 1)
+        def _():
+            give(j // parts_of).start()
 
     def tick(j, _):
         @pl.when(j < chunks)
@@ -216,36 +232,33 @@
 
     lax.fori_loop(0, chunks + LAG, tick, 0)
 
-    def finish(results):
+    for b in range(blocks):
+        @pl.when(jnp.logical_not(is_owner))
+        def _():
+            give(b).wait_recv()
+
+        some = [ag_out[j] for j in range(b * parts_of, (b + 1) * parts_of)]
+        first = jnp.concatenate([r[:WIDE] for r in some])
+        rest = jnp.concatenate([v for r in some for v in (r[WIDE:], turned(r[WIDE:], HALF))])
+        lane = lax.broadcasted_iota(jnp.int32, first.shape, 1)
+        over = LANES - shard
+        second = jnp.where(lane < over, turned(first, over), turned(rest, over))
+        out[b] = jnp.where(core == 0, first, second).T[:shard]
+
+    @pl.when(jnp.logical_not(is_owner))
+    def _():
+        pltpu.make_async_copy(rs_out, rs_out, rs_send).wait()
+
+    @pl.when(is_owner)
+    def _():
         for b in range(blocks):
-            some = [results[b * parts_of + c] for c in range(parts_of)]
-            first = jnp.concatenate([r[:WIDE] for r in some])
-            rest = jnp.concatenate([v for r in some for v in (r[WIDE:], turned(r[WIDE:], HALF))])
-            lane = lax.broadcasted_iota(jnp.int32, first.shape, 1)
-            over = LANES - shard
-            second = jnp.where(lane < over, turned(first, over), turned(rest, over))
-            out[b] = jnp.where(core == 0, first, second).T[:shard]
-
-    @pl.when(is_owner)
-    def _():
-        give = pltpu.make_async_remote_copy(
-            src_ref=ag_out, dst_ref=from_other, send_sem=out_send, recv_sem=out_recv, device_id=sibling,
-            device_id_type=MESH)
-        give.start()
-        finish([ag_out[j] for j in range(chunks)])
-        give.wait_send()
+            give(b).wait_send()
         sent = rs_out.at[:, pl.ds(0, cols - 1)]
         pltpu.make_async_copy(sent, sent, rs_send).wait()
 
-        @pl.when(layer < layers - 1)
-        def _():
-            pltpu.make_async_copy(rs_in, rs_in, ag_send).wait()
-
-    @pl.when(jnp.logical_not(is_owner))
-    def _():
-        pltpu.make_async_copy(from_other, from_other, out_recv).wait()
-        finish([from_other[j] for j in range(chunks)])
-        pltpu.make_async_copy(rs_out, rs_out, rs_send).wait()
+    @pl.when(hands_on)
+    def _():
+        pltpu.make_async_copy(rs_in, rs_in, ag_send).wait()
 
     for swap in swaps:
         swap.wait_send()
@@ -279,9 +292,9 @@
                 pltpu.VMEM((chunks, cols, piece, LANES), F32),
                 pltpu.VMEM((chunks, 2 * cols, piece, LANES), F32),
                 pltpu.VMEM((chunks, piece, LANES), F32),
-                pltpu.VMEM((chunks, piece, LANES), F32),
                 pltpu.VMEM((2, 8, LANES), F32),
                 pltpu.VMEM((piece, LANES), F32),
+                pltpu.SemaphoreType.REGULAR,
                 sems((2,)),
                 sems((depth // LANES + 1,)),
                 sems((depth // LANES + 1,)),
@@ -289,11 +302,11 @@
                 sems((chunks,)),
                 sems,
                 sems((chunks,)),
-                sems,
-                sems,
+                sems((blocks,)),
+                sems((blocks,)),
             ],
             compiler_params=pltpu.CompilerParams(
-                collective_id=0, has_side_effects=True, vmem_limit_bytes=56 * 2**20
+                collective_id=0, has_side_effects=True, vmem_limit_bytes=52 * 2**20
             ),
             name="front_sweep",
         )(

time: 110 us -> 105 us (0.955)
  Pallas kernels: 108 us -> 103 us
    pallas_call x1, Pallas kernels: 108 us -> 103 us  [body(): pl.pallas_call(functools.partial(sweep, (layers, chips, cols)), out_shape...]
where the time goes in v3:
time: 105 us
  Pallas kernels  103 us (98%)
  local copies, waits for them, and re-layouts  1.32 us (1%)
    pallas_call x1, Pallas kernels, body(): pl.pallas_call(functools.partial(sweep, (layers, chips, cols)), out_shape...  103 us

profile of v3, /device:TPU:57, one launch (start us, length us, event | category | flops | bytes accessed | tf_op | source)
XLA Modules:
  0.0 104.8 jit_solution(7306133009667829346)
XLA Ops:
  0.0 0.0 copy-start
  0.0 0.7 copy-done
  0.7 103.5 %front_sweep.1 = f32[3,96,128]{2,1,0:T(8,128)S(1)} custom-call(f32[4608,128]{1,0:T(8,128)} %bitcast.4, f32[1,96]{1,0:T(1,128)S(1)} %copy-done, f32[3,1536,128]{2,1,0:T(8,128)} %bitcast.5), custom_call_target="tpu_custom_call" | custom-call | tf_op jit(solution)/shard_map/front_sweep/pallas_call | solution.py:275
  104.2 0.7 copy.5
Async XLA Ops:
  0.0 0.7 copy-start

commit v4 on v3

--- a/solution.py
+++ b/solution.py
@@ -65,7 +65,7 @@
 
     mine = pl.multiple_of(core * depth, LANES)
     load_src = pltpu.make_async_copy(sources.at[:, pl.ds(mine, depth)], src, load_sem.at[0])
-    load_m = pltpu.make_async_copy(front, tile, load_sem.at[1])
+    load_m = pltpu.make_async_copy(front, tile.at[pl.ds(0, front.shape[0])], load_sem.at[1])
     load_m.start()
     load_src.start()
 
@@ -282,7 +282,7 @@
             ],
             out_specs=pl.BlockSpec(memory_space=pltpu.VMEM),
             scratch_shapes=[
-                pltpu.VMEM((rows * 2 * depth // LANES, LANES), F32),
+                pltpu.VMEM((rows * 2 * depth // LANES + 16, LANES), F32),
                 pltpu.VMEM((rows, depth), F32),
                 pltpu.VMEM((2, rows, depth), F32),
                 pltpu.VMEM((cols // 2, depth, 2 * rows), BF16),

time: 105 us -> 105 us (level)
  no operation moved by 1% of the time
where the time goes in v4:
time: 105 us
  Pallas kernels  104 us (99%)
  local copies, waits for them, and re-layouts  1.32 us (1%)
    pallas_call x1, Pallas kernels, body(): pl.pallas_call(functools.partial(sweep, (layers, chips, cols)), out_shape...  104 us

profile of v4, /device:TPU:57, one launch (start us, length us, event | category | flops | bytes accessed | tf_op | source)
XLA Modules:
  0.0 104.9 jit_solution(2641545255779615796)
XLA Ops:
  0.0 0.0 copy-start
  0.0 0.7 copy-done
  0.7 103.5 %front_sweep.1 = f32[3,96,128]{2,1,0:T(8,128)S(1)} custom-call(f32[4608,128]{1,0:T(8,128)} %bitcast.4, f32[1,96]{1,0:T(1,128)S(1)} %copy-done, f32[3,1536,128]{2,1,0:T(8,128)} %bitcast.5), custom_call_target="tpu_custom_call" | custom-call | tf_op jit(solution)/shard_map/front_sweep/pallas_call | solution.py:275
  104.2 0.7 copy.5
Async XLA Ops:
  0.0 0.7 copy-start

commit v5 on v4

--- a/solution.py
+++ b/solution.py
@@ -163,8 +163,8 @@
         total = own[j] + jnp.concatenate(came, axis=1)
         high = total.astype(BF16)
         vec = jnp.concatenate([high, (total - high.astype(F32)).astype(BF16)])
-        for pair in range(cols // 2):
-            result = jnp.dot(vec, m_parts[pair], preferred_element_type=F32)
+        results = [jnp.dot(vec, m_parts[pair], preferred_element_type=F32) for pair in range(cols // 2)]
+        for pair, result in enumerate(results):
             result = result[:WIDE] + result[WIDE:]
             result = result[:, : 3 * LANES] + result[:, 3 * LANES :]
             top, bottom = result[: WIDE // 2, 2 * LANES :], result[WIDE // 2 :, 2 * LANES :]
@@ -198,9 +198,10 @@
     def hand_on(j):
         arrived = rs_in.at[j, pl.ds(0, 2 * cols - 1)]
         pltpu.make_async_copy(arrived, arrived, rs_recv.at[j]).wait()
-        total = rs_in[j, 0]
-        for s in range(1, 2 * cols):
-            total = total + rs_in[j, s]
+        sums = [rs_in[j, s] for s in range(2 * cols)]
+        while len(sums) > 1:
+            sums = [x + y for x, y in zip(sums[::2], sums[1::2])]
+        total = sums[0]
         ag_out[j] = total * scale[...]
 
         @pl.when(layer < layers - 1)

time: 105 us -> 104 us (level)
  no operation moved by 1% of the time
where the time goes in v5:
time: 104 us
  Pallas kernels  103 us (99%)
  local copies, waits for them, and re-layouts  1.32 us (1%)
    pallas_call x1, Pallas kernels, body(): pl.pallas_call(functools.partial(sweep, (layers, chips, cols)), out_shape...  103 us

profile of v5, /device:TPU:57, one launch (start us, length us, event | category | flops | bytes accessed | tf_op | source)
XLA Modules:
  0.0 104.3 jit_solution(5087387844168616473)
XLA Ops:
  0.0 0.0 copy-start
  0.0 0.7 copy-done
  0.7 102.9 %front_sweep.1 = f32[3,96,128]{2,1,0:T(8,128)S(1)} custom-call(f32[4608,128]{1,0:T(8,128)} %bitcast.4, f32[1,96]{1,0:T(1,128)S(1)} %copy-done, f32[3,1536,128]{2,1,0:T(8,128)} %bitcast.5), custom_call_target="tpu_custom_call" | custom-call | tf_op jit(solution)/shard_map/front_sweep/pallas_call | solution.py:276
  103.6 0.7 copy.5
Async XLA Ops:
  0.0 0.7 copy-start

commit v6 on v5

--- a/solution.py
+++ b/solution.py
@@ -14,7 +14,7 @@
 WIDE = 16
 LAG = 3
 ORDER = (2, 1, 3, 0)
-SPREAD = (4, 3, 5, 2, 6, 1, 7, 0)
+SPREAD = (4, 3, 5, 2, 6, 0, 1, 7)
 
 
 def left(x, y):

time: 104 us -> 104 us (level)
  no operation moved by 1% of the time
where the time goes in v6:
time: 104 us
  Pallas kernels  103 us (99%)
  local copies, waits for them, and re-layouts  1.32 us (1%)
    pallas_call x1, Pallas kernels, body(): pl.pallas_call(functools.partial(sweep, (layers, chips, cols)), out_shape...  103 us

profile of v6, /device:TPU:57, one launch (start us, length us, event | category | flops | bytes accessed | tf_op | source)
XLA Modules:
  0.0 104.2 jit_solution(9574251762834165165)
XLA Ops:
  0.0 0.0 copy-start
  0.0 0.7 copy-done
  0.7 102.9 %front_sweep.1 = f32[3,96,128]{2,1,0:T(8,128)S(1)} custom-call(f32[4608,128]{1,0:T(8,128)} %bitcast.4, f32[1,96]{1,0:T(1,128)S(1)} %copy-done, f32[3,1536,128]{2,1,0:T(8,128)} %bitcast.5), custom_call_target="tpu_custom_call" | custom-call | tf_op jit(solution)/shard_map/front_sweep/pallas_call | solution.py:276
  103.6 0.7 copy.5
Async XLA Ops:
  0.0 0.7 copy-start
